TPU v7x, 256 devices: a whole 4x4x8 slice. The times are simulated.
256 devices in a mesh: dp: 4 (over x), section: 2 (over core), tensor: 32 (over z, y).
Axes of the slice: x: 4, y: 4, z: 8, core: 2. Of those that a mesh axis runs over, the one named last changes fastest.
Arguments:
- base: bfloat16 [4096, 8192], P('dp', 'tensor'), may hold values from -400 to 400
- deltas: bfloat16 [2, 4096, 8192], P('section', 'dp', 'tensor'), may hold values from -6 to 6
- gain: float32 [8192], P('tensor'), may hold values from 0.5 to 1.5
- lengths: int32 [4], replicated, may hold values from 1 to 1024, 2560 in all
Outputs:
- gram: float32 [2, 8192, 8192], P('section', 'dp', 'tensor')
- cross: float32 [2, 8192, 8192], P('section', 'dp', 'tensor')
All inputs are finite; a program needn't handle non-finite values.
Results may differ from a plain program's by a relative error of at most 0.0029.
Values may be sent and summed in bfloat16 or wider, within the bound.
A program may use at most 128 MiB of HBM per device.

v0:
```python
import jax
import jax.numpy as jnp
from jax import lax
from jax.sharding import PartitionSpec as P

D = 8192


def entering(array, axis, join, neutral):
    place = lax.axis_index(axis)
    gathered = lax.all_gather(array.astype(jnp.bfloat16), axis)
    state = jnp.zeros_like(array) + jnp.asarray(neutral, array.dtype)

    def one(step, state):
        return join(state, lax.dynamic_index_in_dim(gathered, step, 0, False).astype(array.dtype))

    return lax.fori_loop(0, place, one, state)


def spread(block, axis, source):
    block = jnp.where(lax.axis_index(axis) == source, block, jnp.zeros_like(block))
    return lax.psum(block, axis)


def normalized(state, squares, live, gain):
    scale = lax.rsqrt(squares[:, None] / D + 1e-05)
    return (live * gain[None, :] * state * scale).astype(jnp.bfloat16)


def shards(base, deltas, gain, lengths):
    rows = base.shape[0]
    cols = base.shape[1]
    group = lax.axis_index("dp")
    live = (jnp.arange(rows, dtype=jnp.int32) < lengths[group]).astype(jnp.float32)[:, None]
    count = jnp.sum(lengths).astype(jnp.float32)
    own = deltas[0].astype(jnp.float32)
    start_state = base.astype(jnp.float32)
    earlier = entering(own, "section", jnp.add, jnp.zeros_like(own))
    state = start_state + earlier + own
    final = spread(state, "section", lax.axis_size("section") - 1)
    state_sq, final_sq = lax.psum(
        (jnp.sum(state * state, axis=1), jnp.sum(final * final, axis=1)), "tensor"
    )
    lens = normalized(state, state_sq, live, gain)
    target = normalized(final, final_sq, live, gain)
    lens_full = lax.all_gather(lens, "tensor", axis=1, tiled=True)
    paired = jnp.concatenate([lens, target], axis=1)
    contract = (((0,), (0,)), ((), ()))
    summed = lax.psum_scatter(
        lax.dot_general(lens_full, paired, contract, preferred_element_type=jnp.float32),
        "dp",
        scatter_dimension=0,
        tiled=True,
    )
    gram = summed[:, :cols] / count
    cross = summed[:, cols:] / count
    return (gram[None], cross[None])


def solution(mesh):
    placed = (P("dp", "tensor"), P("section", "dp", "tensor"), P("tensor"), P())
    return jax.shard_map(
        shards,
        mesh=mesh,
        in_specs=placed,
        out_specs=(P("section", "dp", "tensor"), P("section", "dp", "tensor")),
        check_vma=False,
    )
```

profile of v0, /device:TPU:2, one launch (start us, length us, event | category | flops | bytes accessed | tf_op | source)
XLA Modules:
  0.0 462.1 jit_solution(7293411576929954089)
XLA Ops:
  7.2 0.0 all-gather.3.cloned.1.call-start
  7.2 0.7 all-gather.3.cloned.1.call-update
  7.9 0.0 all-reduce.3.cloned.1.call-start
  7.9 19.2 %all-gather.3.cloned.1.call-done = bf16[2,1024,256]{2,1,0:T(8,128)(2,1)} async-done(((bf16[1,1024,256]{2,1,0:T(8,128)(2,1)}), bf16[2,1024,256]{2,1,0:T(8,128)(2,1)}) %all-gather.3.cloned.1.call-update) | async-done | bytes 1048592 | tf_op jit(solution)/shard_map/all_gather | solution.py:11
  27.1 0.1 broadcast.22
  27.2 0.0 copy-start
  27.2 0.0 copy-start.1
  27.3 1.0 copy-done
  28.3 0.2 copy-done.1
  28.4 0.0 copy-start.3
  28.4 0.0 copy-start.2
  28.4 1.2 broadcast_select_fusion
  29.6 0.0 all-reduce.3.cloned.1.call-update
  29.7 0.0 all-gather.5.cloned.1.call-start
  29.7 0.0 copy-done.3
  29.7 0.6 dynamic_slice.7
  30.3 0.6 fusion.10
  31.0 31.1 %all-reduce.3.cloned.1.call-done = f32[1024,256]{1,0:T(8,128)} async-done(((f32[1024,256]{1,0:T(8,128)}), f32[1024,256]{1,0:T(8,128)}) %all-reduce.3.cloned.1.call-update) | async-done | bytes 1048592 | tf_op jit(solution)/shard_map/psum | solution.py:22
  62.0 1.4 multiply_reduce_fusion
  63.5 76.2 %all-reduce = (f32[1024]{0:T(1024)S(1)}, f32[1024]{0:T(1024)S(1)}) all-reduce(f32[1024]{0:T(1024)S(1)} %get-tuple-element.39, f32[1024]{0:T(1024)S(1)} %multiply_reduce_fusion), channel_id=1, replica_groups=mesh['dp'=4,'section'=2,'tensor'=32] {'tensor'}, use_global_device_ids=true, to_apply=%region_3.4 | all-reduce | flops 2048 | bytes 16384 | tf_op jit(solution)/shard_map/psum | solution.py:41
  139.7 0.0 copy-done.2
  139.7 2.5 fusion.5
  142.2 0.0 all-gather.5.cloned.1.call-update
  142.2 0.0 reduce-scatter.2.cloned.1.call-start
  142.3 146.8 %all-gather.5.cloned.1.call-done = bf16[1024,8192]{1,0:T(8,128)(2,1)} async-done(((bf16[1024,256]{1,0:T(8,128)(2,1)}), bf16[1024,8192]{1,0:T(8,128)(2,1)}) %all-gather.5.cloned.1.call-update) | async-done | bytes 16777232 | tf_op jit(solution)/shard_map/all_gather | solution.py:46
  289.0 15.8 %fusion.6 = f32[8192,512]{1,0:T(8,128)} fusion(bf16[1024,8192]{1,0:T(8,128)(2,1)} %all-gather.5.cloned.1.call-done, bf16[1024,256]{1,0:T(8,128)(2,1)S(1)} %get-tuple-element.40, bf16[1024,256]{1,0:T(8,128)(2,1)} %get-tuple-element.41), kind=kOutput, calls=%fused_computation.11 | convolution fusion | flops 8592031744 | bytes 34603008 | tf_op jit(solution)/shard_map/dot_general | solution.py:50
  304.8 0.0 reduce-scatter.2.cloned.1.call-update
  304.9 0.6 reduce_sum.29
  306.2 144.9 %reduce-scatter.2.cloned.1.call-done = f32[2048,512]{1,0:T(8,128)} async-done(((f32[8192,512]{1,0:T(8,128)}), f32[2048,512]{1,0:T(8,128)}) %reduce-scatter.2.cloned.1.call-update) | async-done | bytes 4194320 | tf_op jit(solution)/shard_map/reduce_scatter | solution.py:49
  451.1 4.5 fusion
  (2 shorter events, 0.0 us)
Async XLA Ops:
  7.2 20.0 %all-gather.3.cloned.1.call-start = ((), (), s32[]{:S(2)}) async-start(), calls=%async_computation.1 | async-start | bytes 1572864 | tf_op jit(solution)/shard_map/all_gather | solution.py:11
  7.9 54.1 %all-reduce.3.cloned.1.call-start = ((), (), s32[]{:S(2)}) async-start(), calls=%async_computation.3 | async-start | bytes 2097152 | tf_op jit(solution)/shard_map/psum | solution.py:22
  27.2 1.0 copy-start
  27.2 1.2 copy-start.1
  28.4 1.3 copy-start.3
  28.4 111.3 %copy-start.2 = (f32[256]{0:T(256)S(1)}, f32[256]{0:T(256)}, u32[]{:S(2)}) copy-start(f32[256]{0:T(256)} %param.8) | copy-start | bytes 3076
  29.7 259.4 %all-gather.5.cloned.1.call-start = ((), (), s32[]{:S(2)}) async-start(), calls=%async_computation.2 | async-start | bytes 17301504 | tf_op jit(solution)/shard_map/all_gather | solution.py:46
  142.2 308.9 %reduce-scatter.2.cloned.1.call-start = ((), (), s32[]{:S(2)}) async-start(), calls=%async_computation.4 | async-start | bytes 20971520 | tf_op jit(solution)/shard_map/reduce_scatter | solution.py:49
Sparse Core Ops, SparseCore 0:
  9.8 17.3 all-gather.2
  30.3 31.6 all-reduce.2
  142.3 146.6 all-gather.4
  305.0 146.0 reduce-scatter.1
where the time goes:
time: 464 us; the launch traced here: 462 us
  waiting for transfers between devices  343 us (74%)
  blocking collectives  76.2 us (16%)
  matrix products  15.8 us (3%)
  between operations  14.5 us (3%)
  other arithmetic  10.9 us (2%)
    all_gather x1, waiting for transfers between devices, shards(): lens_full = lax.all_gather(lens, 'tensor', axis=1, tiled=True)  147 us
    reduce_scatter x1, waiting for transfers between devices, shards(): lax.psum_scatter(lax.dot_general(lens_full, paired, contract, preferred_e...  145 us
    psum x1, blocking collectives, shards(): lax.psum((jnp.sum(state * state, axis=1), jnp.sum(final * final, axis=1))...  76.2 us
    psum x1, waiting for transfers between devices, spread(): return lax.psum(block, axis)  31.1 us
    all_gather x1, waiting for transfers between devices, entering(): gathered = lax.all_gather(array.astype(jnp.bfloat16), axis)  19.2 us
    dot_general x1, matrix products, shards(): lax.dot_general(lens_full, paired, contract, preferred_element_type=jnp.f...  15.8 us
  transfers between devices with their start and end apart: 4, of which 4 were waited for; matrix products, arithmetic and copies ran while one was open for 0% of the time, Pallas kernels for 0%

commit v1 on v0

v1 whole, which is shorter than its diff:
```python
import jax
import jax.numpy as jnp
from jax import lax
from jax.experimental import pallas as pl
from jax.experimental.pallas import tpu as pltpu
from jax.sharding import PartitionSpec as P

D = 8192
T = 1024
F = 256
NX, NY, NZ = 4, 4, 8
MESH = pl.DeviceIdType.MESH
LANE = 128


def kernel(
    len_ref, base, delta, gain, out,
    early, turned, zstat, ystat, rows, cols, sbuf, rbuf, fin,
    early_sem, zstat_sem, ystat_sem, z_sem, y_sem, relay_sem, ring_sem, last_sem, local_sem,
):
    f32, bf16 = jnp.float32, jnp.bfloat16
    x, c, t = lax.axis_index("dp"), lax.axis_index("section"), lax.axis_index("tensor")
    z, y = t // NY, t % NY

    def at_x(k):
        return ((x + k) % NX, c, t)

    def at_y(k):
        return (x, c, z * NY + (y + k) % NY)

    def at_z(k):
        return (x, c, ((z + k) % NZ) * NY + y)

    def copy(src, dst, sems, index, device):
        return pltpu.make_async_remote_copy(
            src_ref=src,
            dst_ref=dst,
            send_sem=sems.at[(0, *index)],
            recv_sem=sems.at[(1, *index)],
            device_id=device,
            device_id_type=MESH,
        )

    other = (x, 1 - c, t)

    barrier = pltpu.get_barrier_semaphore()
    peers = [at_z(k) for k in range(1, NZ)] + [at_y(k) for k in range(1, NY)] + [at_x(1), at_x(3), other]
    for peer in peers:
        pl.semaphore_signal(barrier, inc=1, device_id=peer, device_id_type=MESH)
    pl.semaphore_wait(barrier, len(peers))

    early_copy = copy(delta, early, early_sem, (), other)

    @pl.when(c == 0)
    def _():
        early_copy.start()
        early[...] = jnp.zeros_like(early)

    @pl.when(c == 1)
    def _():
        early_copy.wait_recv()

    for k in range(T // LANE):
        part = slice(k * LANE, (k + 1) * LANE)
        state = base[part, :].astype(f32) + early[part, :].astype(f32) + delta[part, :].astype(f32)
        state = state.T
        turned[:, part] = state
        zstat[z, :, part] = jnp.sum(state * state, axis=0, keepdims=True)

    def zstat_copy(k, slot):
        return copy(zstat.at[slot], zstat.at[slot], zstat_sem, (k,), at_z(k))

    def ystat_copy(k, slot):
        return copy(ystat.at[slot], ystat.at[slot], ystat_sem, (k,), at_y(k))

    for k in range(1, NZ):
        zstat_copy(k, z).start()
    for k in range(1, NZ):
        zstat_copy(k, (z + NZ - k) % NZ).wait_recv()
    total = zstat[0]
    for k in range(1, NZ):
        total = total + zstat[k]
    ystat[y] = total
    for k in range(1, NY):
        ystat_copy(k, y).start()
    for k in range(1, NY):
        ystat_copy(k, (y + NY - k) % NY).wait_recv()
    total = ystat[0]
    for k in range(1, NY):
        total = total + ystat[k]
    slots = lax.broadcasted_iota(jnp.int32, (1, T), 1)
    live = jnp.where(slots < len_ref[x], 1.0, 0.0).astype(f32)
    factor = live * lax.rsqrt(total / D + 1e-05)

    gain_down = jnp.broadcast_to(gain[...], (LANE, F)).T
    for k in range(T // LANE):
        part = slice(k * LANE, (k + 1) * LANE)
        lens = gain_down * turned[:, part] * factor[:, part]
        rows[0, :, part] = lens.astype(bf16)
        cols[0, y, part, :] = lens.T.astype(bf16)

    def z_copy(hop, way):
        if hop < 4:
            src = rows.at[0 if hop == 1 else 2 * hop - 3 + way]
            dst = rows.at[2 * hop - 1 + way]
        else:
            half = pl.ds(way * (F // 2), F // 2)
            src, dst = rows.at[5 + way, half], rows.at[7, half]
        return copy(src, dst, z_sem, (2 * (hop - 1) + way,), at_z(1 - 2 * way))

    def y_copy(hop, way, block):
        ref = cols.at[0, block]
        if hop == 2:
            ref = cols.at[0, block, pl.ds(way * (T // 2), T // 2)]
        return copy(ref, ref, y_sem, (2 * (hop - 1) + way,), at_y(1 - 2 * way))

    def relay(k):
        block = (y + (0, 3, 1, 2)[k]) % NY
        return copy(cols.at[0, block], cols.at[1, block], relay_sem, (k,), other)

    def start_relay(k):
        @pl.when(c == 1)
        def _():
            relay(k).start()

    for way in range(2):
        z_copy(1, way).start()
        y_copy(1, way, y).start()
    start_relay(0)
    for way in range(2):
        z_copy(1, way).wait_recv()
        z_copy(2, way).start()
    before, after, across = (y + 3) % NY, (y + 1) % NY, (y + 2) % NY
    y_copy(1, 0, before).wait_recv()
    y_copy(2, 0, before).start()
    start_relay(1)
    y_copy(1, 1, after).wait_recv()
    y_copy(2, 1, after).start()
    start_relay(2)
    for way in range(2):
        y_copy(2, way, across).wait_recv()
    start_relay(3)

    @pl.when(c == 0)
    def _():
        for k in range(4):
            relay(k).wait_recv()

    def place_of(s):
        m = (s + 1) // 2
        zz = (z + NZ + jnp.where(s % 2 == 1, -m, m)) % NZ
        return zz // 2, zz % 2

    def position(dest, way):
        return jnp.where(way == 0, x + NX - dest - 1, dest + NX - 1 - x) % NX

    units = 4 - 2 * c

    def unit_of(way, j):
        r = jnp.where(c == 0, j, 2 * way + j)
        hop = jnp.where(r == 0, 0, jnp.where(r == 3, 2, jnp.where(r == 1, 3, 1)))
        return 4 * way + j, way * (1 - c), hop

    def ring_copy(s, u, way):
        return copy(sbuf.at[s, u], rbuf.at[s, u], ring_sem, (s, u), at_x(jnp.where(way == 0, 1, 3)))

    def last_rows(b, block):
        return pl.ds(pl.multiple_of(b * (NY * F) + block * F, F), F)

    def last_copy(k, b, layer, u, block):
        return copy(fin.at[b, u], out.at[layer, last_rows(b, block)], last_sem, (k, b, layer), at_y(k))

    def local_copy(b, layer, u):
        return pltpu.make_async_copy(fin.at[b, u], out.at[layer, last_rows(b, y)], local_sem.at[b, layer])

    def work(s, p, way):
        dest, b = place_of(s)

        def one(j, carry):
            u, layer, hop = unit_of(way, j)
            acc = jnp.dot(rows[s], cols[layer, (y + hop) % NY], preferred_element_type=f32)
            if p > 0:
                ring_copy(s, u, way).wait_recv()
                acc = acc + rbuf[s, u].astype(f32)
            if p < 3:
                sbuf[s, u] = acc.astype(bf16)
                ring_copy(s, u, way).start()
            else:
                fin[b, u] = acc

                @pl.when(hop == 0)
                def _():
                    local_copy(b, layer, u).start()

                @pl.when(hop != 0)
                def _():
                    last_copy(hop, b, layer, u, y).start()

            return carry

        lax.fori_loop(0, units, one, 0)

    def step(tau, carry):
        for hop in (2, 3, 4):

            @pl.when(tau == hop)
            def _(hop=hop):
                for way in range(2):
                    z_copy(hop, way).wait_recv()
                    if hop < 4:
                        z_copy(hop + 1, way).start()

        for p in range(4):

            def one(k, carry, p=p):
                s = 2 * (tau - p) - 1 + k // 2
                way = k % 2

                @pl.when((s >= 0) & (s < NZ))
                def _():
                    dest, _b = place_of(s)

                    @pl.when(position(dest, way) == p)
                    def _():
                        work(s, p, way)

                return carry

            lax.fori_loop(0, 4, one, 0)
        return carry

    lax.fori_loop(0, 8, step, 0)

    def ending(k, carry):
        b, layer = k % 2, k // 2
        for hop in range(1, NY):
            last_copy(hop, b, layer, 0, (y + NY - hop) % NY).wait_recv()
            last_copy(hop, b, layer, 0, y).wait_send()
        local_copy(b, layer, 0).wait()
        return carry

    lax.fori_loop(0, 2 * (2 - c), ending, 0)

    def sent(k, carry):
        s, way = k // 2, k % 2
        dest, _b = place_of(s)

        @pl.when(position(dest, way) < 3)
        def _():
            def one(j, carry):
                ring_copy(s, 4 * way + j, way).wait_send()
                return carry

            lax.fori_loop(0, units, one, 0)

        return carry

    lax.fori_loop(0, 2 * NZ, sent, 0)
    for k in range(1, NZ):
        zstat_copy(k, z).wait_send()
    for k in range(1, NY):
        ystat_copy(k, y).wait_send()
    for way in range(2):
        for hop in range(1, 5):
            z_copy(hop, way).wait_send()
        y_copy(1, way, y).wait_send()
        y_copy(2, way, (before, after)[way]).wait_send()

    @pl.when(c == 0)
    def _():
        early_copy.wait_send()

    @pl.when(c == 1)
    def _():
        for k in range(4):
            relay(k).wait_send()


def products(lengths, base, delta, gain):
    f32, bf16 = jnp.float32, jnp.bfloat16
    dma = pltpu.SemaphoreType.DMA
    vmem = pl.BlockSpec(memory_space=pltpu.VMEM)
    return pl.pallas_call(
        kernel,
        out_shape=jax.ShapeDtypeStruct((2, 2 * NY * F, F), f32),
        in_specs=[pl.BlockSpec(memory_space=pltpu.SMEM), vmem, vmem, vmem],
        out_specs=pl.BlockSpec(memory_space=pl.ANY),
        scratch_shapes=[
            pltpu.VMEM((T, F), bf16),
            pltpu.VMEM((F, T), f32),
            pltpu.VMEM((NZ, 1, T), f32),
            pltpu.VMEM((NY, 1, T), f32),
            pltpu.VMEM((NZ, F, T), bf16),
            pltpu.VMEM((2, NY, T, F), bf16),
            pltpu.VMEM((NZ, 8, F, F), bf16),
            pltpu.VMEM((NZ, 8, F, F), bf16),
            pltpu.VMEM((2, 8, F, F), f32),
            dma((2,)),
            dma((2, NZ)),
            dma((2, NY)),
            dma((2, 8)),
            dma((2, 4)),
            dma((2, 4)),
            dma((2, NZ, 8)),
            dma((2, NY, 2, 2)),
            dma((2, 2)),
        ],
        compiler_params=pltpu.CompilerParams(
            collective_id=0, has_side_effects=True, vmem_limit_bytes=48 * 1024 * 1024
        ),
        cost_estimate=pl.CostEstimate(flops=8 * 2 * F * T * 2048, bytes_accessed=8 << 20, transcendentals=0),
    )(lengths, base, delta, gain)


def shards(base, deltas, gain, lengths):
    count = jnp.sum(lengths).astype(jnp.float32)
    summed = products(lengths, base, deltas[0], gain[None, :])
    gram = summed[0] / count
    cross = jnp.where(lax.axis_index("section") == 0, summed[1], summed[0]) / count
    return gram[None], cross[None]


def solution(mesh):
    placed = (P("dp", "tensor"), P("section", "dp", "tensor"), P("tensor"), P())
    return jax.shard_map(
        shards,
        mesh=mesh,
        in_specs=placed,
        out_specs=(P("section", "dp", "tensor"), P("section", "dp", "tensor")),
        check_vma=False,
    )
```

time: 464 us -> 136 us (0.29)
  waiting for transfers between devices: 343 us -> 0 us
  Pallas kernels: 0 us -> 126 us
  blocking collectives: 76.2 us -> 0 us
  matrix products: 15.8 us -> 0 us
  between operations: 14.5 us -> 1.31 us
  other arithmetic: 10.9 us -> 3.59 us
    all_gather x2 -> x0, waiting for transfers between devices: 166 us -> none  [the longest x1 147 us: shards(): lens_full = lax.all_gather(lens, 'tensor', axis=1, tiled=True)]
    reduce_scatter x1 -> x0, waiting for transfers between devices: 145 us -> none  [shards(): lax.psum_scatter(lax.dot_general(lens_full, paired, contract, preferred_e...]
    pallas_call x0 -> x1, Pallas kernels: none -> 126 us  [products(): pl.pallas_call(kernel, out_shape=jax.ShapeDtypeStruct((2, 2 * NY * F, F),...]
    psum x1 -> x0, blocking collectives: 76.2 us -> none  [shards(): lax.psum((jnp.sum(state * state, axis=1), jnp.sum(final * final, axis=1))...]
    psum x1 -> x0, waiting for transfers between devices: 31.1 us -> none  [spread(): return lax.psum(block, axis)]
    dot_general x1 -> x0, matrix products: 15.8 us -> none  [shards(): lax.dot_general(lens_full, paired, contract, preferred_element_type=jnp.f...]
  transfers between devices with their start and end apart: 4 -> 0, of which waited for: 4 -> 0; matrix products, arithmetic and copies ran while one was open for 0% -> 0% of each run, Pallas kernels for 0% -> 0%
where the time goes in v1:
time: 136 us; the launch traced here: 135 us
  Pallas kernels  126 us (93%)
  other arithmetic  3.59 us (3%)
  local copies, waits for them, and re-layouts  3.41 us (3%)
    pallas_call x1, Pallas kernels, products(): pl.pallas_call(kernel, out_shape=jax.ShapeDtypeStruct((2, 2 * NY * F, F),...  126 us
    unnamed x8, local copies, waits for them, and re-layouts  3.41 us

profile of v1, /device:TPU:2, one launch (start us, length us, event | category | flops | bytes accessed | tf_op | source)
XLA Modules:
  0.0 134.6 jit_solution(14554978102757693727)
XLA Ops:
  0.6 1.3 reduce_sum.9
  2.6 0.0 copy-start
  2.6 1.0 copy-done
  3.6 0.0 copy-start.1
  3.6 1.0 copy-done.1
  4.7 0.0 copy-start.2
  4.7 0.7 copy-done.2
  5.3 0.0 copy-start.3
  5.3 0.7 copy-done.3
  6.0 126.3 %shard_map.59 = f32[2,2048,256]{2,1,0:T(8,128)S(1)} custom-call(s32[4]{0:T(128)S(1)} %copy-done.3, bf16[1024,256]{1,0:T(8,128)(2,1)S(1)} %copy-done, bf16[1024,256]{1,0:T(8,128)(2,1)S(1)} %bitcast.2, f32[1,256]{1,0:T(1,128)S(1)} %bitcast.3), custom_call_target="tpu_custom_call" | custom-call | flops 8589934592 | bytes 8388608 | tf_op jit(solution)/shard_map/pallas_call | solution.py:283
  132.3 2.3 %select_divide_fusion = (f32[1,2048,256]{2,1,0:T(8,128)}, f32[1,2048,256]{2,1,0:T(8,128)}) fusion(f32[2,2048,256]{2,1,0:T(8,128)S(1)} %shard_map.59, f32[]{:T(128)S(6)} %convert_element_type.3, pred[]{:T(512)S(6)} %eq.3), kind=kLoop, calls=%fused_computation | loop fusion | flops 1572864 | bytes 8388613 | tf_op jit(solution)/shard_map/div | solution.py:319
Async XLA Ops:
  2.6 1.0 copy-start
  3.6 1.0 copy-start.1
  4.7 0.7 copy-start.2
  5.3 0.7 copy-start.3

commit v2 on v1

--- a/solution.py
+++ b/solution.py
@@ -11,12 +11,13 @@
 NX, NY, NZ = 4, 4, 8
 MESH = pl.DeviceIdType.MESH
 LANE = 128
+NEAR, FAR, LATE = 2, 4, 3
 
 
 def kernel(
-    len_ref, base, delta, gain, out,
-    early, turned, zstat, ystat, rows, cols, sbuf, rbuf, fin,
-    early_sem, zstat_sem, ystat_sem, z_sem, y_sem, relay_sem, ring_sem, last_sem, local_sem,
+    len_hbm, base_hbm, delta_hbm, gain_hbm, out,
+    len_ref, base, delta, gain, early, turned, zstat, ystat, rows, cols, sbuf, rbuf, fin,
+    early_sem, zstat_sem, ystat_sem, z_sem, y_sem, relay_sem, ring_sem, last_sem, local_sem, in_sem,
 ):
     f32, bf16 = jnp.float32, jnp.bfloat16
     x, c, t = lax.axis_index("dp"), lax.axis_index("section"), lax.axis_index("tensor")
@@ -43,18 +44,28 @@
 
     other = (x, 1 - c, t)
 
+    fetches = [
+        pltpu.make_async_copy(src, dst, in_sem.at[k])
+        for k, (src, dst) in enumerate(((base_hbm, base), (delta_hbm, delta), (gain_hbm, gain), (len_hbm, len_ref)))
+    ]
+    for fetch in fetches:
+        fetch.start()
+
     barrier = pltpu.get_barrier_semaphore()
     peers = [at_z(k) for k in range(1, NZ)] + [at_y(k) for k in range(1, NY)] + [at_x(1), at_x(3), other]
     for peer in peers:
         pl.semaphore_signal(barrier, inc=1, device_id=peer, device_id_type=MESH)
     pl.semaphore_wait(barrier, len(peers))
 
-    early_copy = copy(delta, early, early_sem, (), other)
+    early_copy = copy(delta_hbm, early, early_sem, (), other)
 
     @pl.when(c == 0)
     def _():
         early_copy.start()
         early[...] = jnp.zeros_like(early)
+
+    for fetch in fetches:
+        fetch.wait()
 
     @pl.when(c == 1)
     def _():
@@ -90,6 +101,7 @@
         total = total + ystat[k]
     slots = lax.broadcasted_iota(jnp.int32, (1, T), 1)
     live = jnp.where(slots < len_ref[x], 1.0, 0.0).astype(f32)
+    count = (len_ref[0] + len_ref[1] + len_ref[2] + len_ref[3]).astype(f32)
     factor = live * lax.rsqrt(total / D + 1e-05)
 
     gain_down = jnp.broadcast_to(gain[...], (LANE, F)).T
@@ -123,28 +135,42 @@
         def _():
             relay(k).start()
 
+    before, after, across = (y + 3) % NY, (y + 1) % NY, (y + 2) % NY
+
+    def rows_out():
+        for way in range(2):
+            z_copy(1, way).start()
+
     for way in range(2):
-        z_copy(1, way).start()
         y_copy(1, way, y).start()
     start_relay(0)
-    for way in range(2):
-        z_copy(1, way).wait_recv()
-        z_copy(2, way).start()
-    before, after, across = (y + 3) % NY, (y + 1) % NY, (y + 2) % NY
-    y_copy(1, 0, before).wait_recv()
-    y_copy(2, 0, before).start()
-    start_relay(1)
-    y_copy(1, 1, after).wait_recv()
-    y_copy(2, 1, after).start()
-    start_relay(2)
-    for way in range(2):
-        y_copy(2, way, across).wait_recv()
-    start_relay(3)
-
-    @pl.when(c == 0)
-    def _():
-        for k in range(4):
-            relay(k).wait_recv()
+    pl.when(c == 0)(rows_out)
+
+    def rows_in(hop):
+        for way in range(2):
+            z_copy(hop, way).wait_recv()
+            if hop < 4:
+                z_copy(hop + 1, way).start()
+
+    def columns_near():
+        y_copy(1, 0, before).wait_recv()
+        y_copy(2, 0, before).start()
+        y_copy(1, 1, after).wait_recv()
+        y_copy(2, 1, after).start()
+        start_relay(1)
+        start_relay(2)
+        pl.when(c == 1)(rows_out)
+
+    def columns_far():
+        for way in range(2):
+            y_copy(2, way, across).wait_recv()
+        start_relay(3)
+
+    def relayed(*ks):
+        @pl.when(c == 0)
+        def _():
+            for k in ks:
+                relay(k).wait_recv()
 
     def place_of(s):
         m = (s + 1) // 2
@@ -173,10 +199,11 @@
     def local_copy(b, layer, u):
         return pltpu.make_async_copy(fin.at[b, u], out.at[layer, last_rows(b, y)], local_sem.at[b, layer])
 
-    def work(s, p, way):
+    def work(s, p, way, first, last):
         dest, b = place_of(s)
 
-        def one(j, carry):
+        def one(r, carry):
+            j = jnp.where(c == 0, r, r - 2 * way)
             u, layer, hop = unit_of(way, j)
             acc = jnp.dot(rows[s], cols[layer, (y + hop) % NY], preferred_element_type=f32)
             if p > 0:
@@ -186,7 +213,7 @@
                 sbuf[s, u] = acc.astype(bf16)
                 ring_copy(s, u, way).start()
             else:
-                fin[b, u] = acc
+                fin[b, u] = (acc / count).astype(bf16)
 
                 @pl.when(hop == 0)
                 def _():
@@ -198,38 +225,56 @@
 
             return carry
 
-        lax.fori_loop(0, units, one, 0)
+        lax.fori_loop(first, last, one, 0)
+
+    def columns_by(a):
+        return jnp.where(a < NEAR, 1, jnp.where(a < FAR, 3, 4))
+
+    def rows_at(s):
+        m = (s + 1) // 2
+        return m + jnp.where((c == 1) & (m > 0), LATE, 0)
 
     def step(tau, carry):
-        for hop in (2, 3, 4):
-
-            @pl.when(tau == hop)
+        for hop in range(1, 5):
+
+            @pl.when(tau == rows_at(2 * hop - 1))
             def _(hop=hop):
-                for way in range(2):
-                    z_copy(hop, way).wait_recv()
-                    if hop < 4:
-                        z_copy(hop + 1, way).start()
+                rows_in(hop)
+
+        @pl.when(tau == NEAR)
+        def _():
+            columns_near()
+            relayed(1, 2)
+
+        @pl.when(tau == FAR)
+        def _():
+            columns_far()
+            relayed(3)
 
         for p in range(4):
-
-            def one(k, carry, p=p):
-                s = 2 * (tau - p) - 1 + k // 2
-                way = k % 2
-
-                @pl.when((s >= 0) & (s < NZ))
+            a = tau - p
+            m = jnp.maximum(jnp.minimum(jnp.where(c == 1, a - LATE, a), 4), 0)
+            s_to = jnp.minimum(2 * m + 1, NZ)
+            s_from = jnp.where((a == NEAR) | (a == FAR), 0, jnp.maximum(2 * m - 1, 0))
+            upto, already = columns_by(a), jnp.where(a == 0, 0, columns_by(a - 1))
+
+            def one(k, carry, p=p, a=a, upto=upto, already=already):
+                s, way = k // 2, k % 2
+                dest, _b = place_of(s)
+
+                @pl.when((a >= 0) & (a <= 4 + LATE) & (position(dest, way) == p))
                 def _():
-                    dest, _b = place_of(s)
-
-                    @pl.when(position(dest, way) == p)
-                    def _():
-                        work(s, p, way)
+                    first = jnp.where(rows_at(s) == a, 0, already)
+                    low, high = jnp.where(c == 0, 0, 2 * way), jnp.where(c == 0, 4, 2 * way + 2)
+                    work(s, p, way, jnp.maximum(first, low), jnp.minimum(upto, high))
 
                 return carry
 
-            lax.fori_loop(0, 4, one, 0)
+            lax.fori_loop(2 * s_from, 2 * s_to, one, 0)
         return carry
 
-    lax.fori_loop(0, 8, step, 0)
+    relayed(0)
+    lax.fori_loop(0, 4 + LATE + 4, step, 0)
 
     def ending(k, carry):
         b, layer = k % 2, k // 2
@@ -279,13 +324,16 @@
 def products(lengths, base, delta, gain):
     f32, bf16 = jnp.float32, jnp.bfloat16
     dma = pltpu.SemaphoreType.DMA
-    vmem = pl.BlockSpec(memory_space=pltpu.VMEM)
     return pl.pallas_call(
         kernel,
-        out_shape=jax.ShapeDtypeStruct((2, 2 * NY * F, F), f32),
-        in_specs=[pl.BlockSpec(memory_space=pltpu.SMEM), vmem, vmem, vmem],
+        out_shape=jax.ShapeDtypeStruct((2, 2 * NY * F, F), bf16),
+        in_specs=[pl.BlockSpec(memory_space=pl.ANY)] * 4,
         out_specs=pl.BlockSpec(memory_space=pl.ANY),
         scratch_shapes=[
+            pltpu.SMEM((NX,), jnp.int32),
+            pltpu.VMEM((T, F), bf16),
+            pltpu.VMEM((T, F), bf16),
+            pltpu.VMEM((1, F), f32),
             pltpu.VMEM((T, F), bf16),
             pltpu.VMEM((F, T), f32),
             pltpu.VMEM((NZ, 1, T), f32),
@@ -294,7 +342,7 @@
             pltpu.VMEM((2, NY, T, F), bf16),
             pltpu.VMEM((NZ, 8, F, F), bf16),
             pltpu.VMEM((NZ, 8, F, F), bf16),
-            pltpu.VMEM((2, 8, F, F), f32),
+            pltpu.VMEM((2, 8, F, F), bf16),
             dma((2,)),
             dma((2, NZ)),
             dma((2, NY)),
@@ -304,6 +352,7 @@
             dma((2, NZ, 8)),
             dma((2, NY, 2, 2)),
             dma((2, 2)),
+            dma((4,)),
         ],
         compiler_params=pltpu.CompilerParams(
             collective_id=0, has_side_effects=True, vmem_limit_bytes=48 * 1024 * 1024
@@ -313,10 +362,9 @@
 
 
 def shards(base, deltas, gain, lengths):
-    count = jnp.sum(lengths).astype(jnp.float32)
-    summed = products(lengths, base, deltas[0], gain[None, :])
-    gram = summed[0] / count
-    cross = jnp.where(lax.axis_index("section") == 0, summed[1], summed[0]) / count
+    summed = products(lengths, base, deltas[0], gain[None, :]).astype(jnp.float32)
+    gram = summed[0]
+    cross = jnp.where(lax.axis_index("section") == 0, summed[1], summed[0])
     return gram[None], cross[None]
 
 

time: 136 us -> 122 us (0.90)
  Pallas kernels: 126 us -> 114 us
    pallas_call x1, Pallas kernels: 126 us -> 114 us  [products(): pl.pallas_call(kernel, out_shape=jax.ShapeDtypeStruct((2, 2 * NY * F, F),...]
    select_n x0 -> x1, other arithmetic: none -> 2.32 us  [shards(): cross = jnp.where(lax.axis_index('section') == 0, summed[1], summed[0])]
    div x1 -> x0, other arithmetic: 2.29 us -> none  [shards(): jnp.where(lax.axis_index('section') == 0, summed[1], summed[0]) / count]
where the time goes in v2:
time: 122 us; the launch traced here: 120 us
  Pallas kernels  114 us (93%)
  local copies, waits for them, and re-layouts  3.41 us (3%)
  other arithmetic  2.64 us (2%)
    pallas_call x1, Pallas kernels, products(): pl.pallas_call(kernel, out_shape=jax.ShapeDtypeStruct((2, 2 * NY * F, F),...  114 us
    unnamed x8, local copies, waits for them, and re-layouts  3.41 us

profile of v2, /device:TPU:2, one launch (start us, length us, event | category | flops | bytes accessed | tf_op | source)
XLA Modules:
  0.0 120.3 jit_solution(12616409986412614820)
XLA Ops:
  0.6 0.0 copy-start
  0.6 1.0 copy-done
  1.7 0.0 copy-start.1
  1.7 1.0 copy-done.1
  2.7 0.0 copy-start.2
  2.7 0.7 copy-done.2
  3.4 0.0 copy-start.3
  3.4 0.7 copy-done.3
  4.1 113.6 %shard_map.59 = bf16[2,2048,256]{2,1,0:T(8,128)(2,1)S(1)} custom-call(s32[4]{0:T(128)S(1)} %copy-done.3, bf16[1024,256]{1,0:T(8,128)(2,1)S(1)} %copy-done, bf16[1024,256]{1,0:T(8,128)(2,1)S(1)} %bitcast.2, f32[1,256]{1,0:T(1,128)S(1)} %bitcast.3), custom_call_target="tpu_custom_call" | custom-call | flops 8589934592 | bytes 8388608 | tf_op jit(solution)/shard_map/pallas_call | solution.py:327
  117.6 0.3 convert_element_type.3
  118.0 2.3 %slice_select_fusion = (f32[1,2048,256]{2,1,0:T(8,128)}, f32[1,2048,256]{2,1,0:T(8,128)}) fusion(f32[2,2048,256]{2,1,0:T(8,128)S(1)} %convert_element_type.3, pred[]{:T(512)S(6)} %eq.3, bf16[2,2048,256]{2,1,0:T(8,128)(2,1)S(1)} %shard_map.59), kind=kLoop, calls=%fused_computation | loop fusion | flops 524288 | bytes 8388609 | tf_op jit(solution)/shard_map/jit(_where)/select_n | solution.py:367
Async XLA Ops:
  0.6 1.0 copy-start
  1.7 1.0 copy-start.1
  2.7 0.7 copy-start.2
  3.4 0.7 copy-start.3

commit v3 on v2

--- a/solution.py
+++ b/solution.py
@@ -11,12 +11,16 @@
 NX, NY, NZ = 4, 4, 8
 MESH = pl.DeviceIdType.MESH
 LANE = 128
-NEAR, FAR, LATE = 2, 4, 3
+ROWS = ((0, 2, 3, 6, 7), (0, 2, 6, 8, 9))
+COLUMNS = ((6, 7), (3, 6))
+LAGS = ((0, 1, 2, 4), (0, 1, 2, 4))
+START = 0
+STEPS = 1 + max(max(max(ROWS[k]), max(COLUMNS[k])) + LAGS[k][3] for k in range(2))
 
 
 def kernel(
     len_hbm, base_hbm, delta_hbm, gain_hbm, out,
-    len_ref, base, delta, gain, early, turned, zstat, ystat, rows, cols, sbuf, rbuf, fin,
+    len_ref, base, delta, gain, early, turned, zstat, ystat, rows, cols, sbuf, rbuf, fin, own,
     early_sem, zstat_sem, ystat_sem, z_sem, y_sem, relay_sem, ring_sem, last_sem, local_sem, in_sem,
 ):
     f32, bf16 = jnp.float32, jnp.bfloat16
@@ -159,7 +163,6 @@
         y_copy(2, 1, after).start()
         start_relay(1)
         start_relay(2)
-        pl.when(c == 1)(rows_out)
 
     def columns_far():
         for way in range(2):
@@ -199,16 +202,26 @@
     def local_copy(b, layer, u):
         return pltpu.make_async_copy(fin.at[b, u], out.at[layer, last_rows(b, y)], local_sem.at[b, layer])
 
-    def work(s, p, way, first, last):
-        dest, b = place_of(s)
-
+    def multiply(s, starts, way, first, last):
         def one(r, carry):
-            j = jnp.where(c == 0, r, r - 2 * way)
-            u, layer, hop = unit_of(way, j)
+            u, layer, hop = unit_of(way, jnp.where(c == 0, r, r - 2 * way))
             acc = jnp.dot(rows[s], cols[layer, (y + hop) % NY], preferred_element_type=f32)
-            if p > 0:
-                ring_copy(s, u, way).wait_recv()
-                acc = acc + rbuf[s, u].astype(f32)
+            if starts:
+                sbuf[s, u] = acc.astype(bf16)
+                ring_copy(s, u, way).start()
+            else:
+                own[s, u] = acc
+            return carry
+
+        lax.fori_loop(first, last, one, 0)
+
+    def add(s, p, way, first, last):
+        _dest, b = place_of(s)
+
+        def one(r, carry):
+            u, layer, hop = unit_of(way, jnp.where(c == 0, r, r - 2 * way))
+            ring_copy(s, u, way).wait_recv()
+            acc = own[s, u] + rbuf[s, u].astype(f32)
             if p < 3:
                 sbuf[s, u] = acc.astype(bf16)
                 ring_copy(s, u, way).start()
@@ -227,46 +240,65 @@
 
         lax.fori_loop(first, last, one, 0)
 
+    def mine(pair):
+        return jnp.where(c == 0, pair[0], pair[1])
+
+    rows_step = [mine([way[g] for way in ROWS]) for g in range(5)]
+    near, far = [mine([way[k] for way in COLUMNS]) for k in range(2)]
+
     def columns_by(a):
-        return jnp.where(a < NEAR, 1, jnp.where(a < FAR, 3, 4))
+        return jnp.where(a < near, 1, jnp.where(a < far, 3, 4))
 
     def rows_at(s):
         m = (s + 1) // 2
-        return m + jnp.where((c == 1) & (m > 0), LATE, 0)
+        at = rows_step[0]
+        for g in range(1, 5):
+            at = jnp.where(m == g, rows_step[g], at)
+        return at
 
     def step(tau, carry):
+        @pl.when((c == 1) & (tau == START))
+        def _():
+            rows_out()
+
+        @pl.when(tau == near)
+        def _():
+            columns_near()
+            relayed(1, 2)
+
+        @pl.when(tau == far)
+        def _():
+            columns_far()
+            relayed(3)
+
         for hop in range(1, 5):
 
-            @pl.when(tau == rows_at(2 * hop - 1))
+            @pl.when(tau == rows_step[hop])
             def _(hop=hop):
                 rows_in(hop)
 
-        @pl.when(tau == NEAR)
-        def _():
-            columns_near()
-            relayed(1, 2)
-
-        @pl.when(tau == FAR)
-        def _():
-            columns_far()
-            relayed(3)
-
-        for p in range(4):
-            a = tau - p
-            m = jnp.maximum(jnp.minimum(jnp.where(c == 1, a - LATE, a), 4), 0)
-            s_to = jnp.minimum(2 * m + 1, NZ)
-            s_from = jnp.where((a == NEAR) | (a == FAR), 0, jnp.maximum(2 * m - 1, 0))
-            upto, already = columns_by(a), jnp.where(a == 0, 0, columns_by(a - 1))
-
-            def one(k, carry, p=p, a=a, upto=upto, already=already):
+        for turn in range(5):
+            p = turn % 4
+            a = tau - mine([way[p] for way in LAGS])
+            before_a = sum(jnp.where(at < a, 1, 0) for at in rows_step)
+            by_a = sum(jnp.where(at <= a, 1, 0) for at in rows_step)
+            s_from = jnp.where((a == near) | (a == far), 0, jnp.maximum(2 * before_a - 1, 0))
+            s_to = jnp.minimum(jnp.maximum(2 * by_a - 1, 0), NZ)
+            upto, already = columns_by(a), columns_by(a - 1)
+
+            def one(k, carry, turn=turn, p=p, a=a, upto=upto, already=already):
                 s, way = k // 2, k % 2
-                dest, _b = place_of(s)
-
-                @pl.when((a >= 0) & (a <= 4 + LATE) & (position(dest, way) == p))
+                at = position(place_of(s)[0], way)
+
+                @pl.when(at > 0 if turn == 4 else at == p)
                 def _():
                     first = jnp.where(rows_at(s) == a, 0, already)
                     low, high = jnp.where(c == 0, 0, 2 * way), jnp.where(c == 0, 4, 2 * way + 2)
-                    work(s, p, way, jnp.maximum(first, low), jnp.minimum(upto, high))
+                    first, last = jnp.maximum(first, low), jnp.minimum(upto, high)
+                    if p == 0:
+                        multiply(s, turn == 0, way, first, last)
+                    else:
+                        add(s, p, way, first, last)
 
                 return carry
 
@@ -274,7 +306,7 @@
         return carry
 
     relayed(0)
-    lax.fori_loop(0, 4 + LATE + 4, step, 0)
+    lax.fori_loop(0, STEPS, step, 0)
 
     def ending(k, carry):
         b, layer = k % 2, k // 2
@@ -343,6 +375,7 @@
             pltpu.VMEM((NZ, 8, F, F), bf16),
             pltpu.VMEM((NZ, 8, F, F), bf16),
             pltpu.VMEM((2, 8, F, F), bf16),
+            pltpu.VMEM((NZ, 8, F, F), f32),
             dma((2,)),
             dma((2, NZ)),
             dma((2, NY)),
@@ -355,7 +388,7 @@
             dma((4,)),
         ],
         compiler_params=pltpu.CompilerParams(
-            collective_id=0, has_side_effects=True, vmem_limit_bytes=48 * 1024 * 1024
+            collective_id=0, has_side_effects=True, vmem_limit_bytes=62 * 1024 * 1024
         ),
         cost_estimate=pl.CostEstimate(flops=8 * 2 * F * T * 2048, bytes_accessed=8 << 20, transcendentals=0),
     )(lengths, base, delta, gain)

time: 122 us -> 118 us (0.967); the launches traced: 120 us -> 118 us
  local copies, waits for them, and re-layouts: 3.41 us -> 0.14 us
  Pallas kernels: 114 us -> 112 us
  other arithmetic: 2.64 us -> 4.38 us
    unnamed x8 -> x2, local copies, waits for them, and re-layouts: 3.41 us -> 0.14 us
    convert_element_type x1, other arithmetic: 0.33 us -> 2.07 us  [shards(): products(lengths, base, deltas[0], gain[None, :]).astype(jnp.float32)]
where the time goes in v3:
time: 118 us
  Pallas kernels  112 us (95%)
  other arithmetic  4.38 us (4%)
    pallas_call x1, Pallas kernels, products(): pl.pallas_call(kernel, out_shape=jax.ShapeDtypeStruct((2, 2 * NY * F, F),...  112 us

profile of v3, /device:TPU:2, one launch (start us, length us, event | category | flops | bytes accessed | tf_op | source)
XLA Modules:
  0.0 117.5 jit_solution(9669837033110648251)
XLA Ops:
  0.6 112.4 %shard_map.59 = bf16[2,2048,256]{2,1,0:T(8,128)(2,1)} custom-call(s32[4]{0:T(128)} %len_hbm.1, bf16[1024,256]{1,0:T(8,128)(2,1)} %base_hbm.1, bf16[1024,256]{1,0:T(8,128)(2,1)} %bitcast.2, f32[1,256]{1,0:T(1,128)} %bitcast.3), custom_call_target="tpu_custom_call" | custom-call | flops 8589934592 | bytes 8388608 | tf_op jit(solution)/shard_map/pallas_call | solution.py:359
  113.0 0.0 copy-start
  113.0 2.1 %convert_element_type.3 = f32[2,2048,256]{2,1,0:T(8,128)S(1)} convert(bf16[2,2048,256]{2,1,0:T(8,128)(2,1)} %shard_map.59) | non-fusion elementwise | flops 1048576 | bytes 6291456 | tf_op jit(solution)/shard_map/convert_element_type | solution.py:398
  115.1 0.1 copy-done
  115.2 2.3 %slice_select_fusion = (f32[1,2048,256]{2,1,0:T(8,128)}, f32[1,2048,256]{2,1,0:T(8,128)}) fusion(f32[2,2048,256]{2,1,0:T(8,128)S(1)} %convert_element_type.3, pred[]{:T(512)S(6)} %eq.3, bf16[2,2048,256]{2,1,0:T(8,128)(2,1)S(1)} %copy-done), kind=kLoop, calls=%fused_computation | loop fusion | flops 524288 | bytes 8388609 | tf_op jit(solution)/shard_map/jit(_where)/select_n | solution.py:400
Async XLA Ops:
  113.0 2.2 %copy-start = (bf16[2,2048,256]{2,1,0:T(8,128)(2,1)S(1)}, bf16[2,2048,256]{2,1,0:T(8,128)(2,1)}, u32[]{:S(2)}) copy-start(bf16[2,2048,256]{2,1,0:T(8,128)(2,1)} %shard_map.59) | copy-start | bytes 6291460

commit v4 on v3

--- a/solution.py
+++ b/solution.py
@@ -203,17 +203,28 @@
         return pltpu.make_async_copy(fin.at[b, u], out.at[layer, last_rows(b, y)], local_sem.at[b, layer])
 
     def multiply(s, starts, way, first, last):
-        def one(r, carry):
-            u, layer, hop = unit_of(way, jnp.where(c == 0, r, r - 2 * way))
-            acc = jnp.dot(rows[s], cols[layer, (y + hop) % NY], preferred_element_type=f32)
-            if starts:
-                sbuf[s, u] = acc.astype(bf16)
-                ring_copy(s, u, way).start()
-            else:
-                own[s, u] = acc
+        def some(r, n):
+            places = [unit_of(way, jnp.where(c == 0, r + k, r + k - 2 * way)) for k in range(n)]
+            accs = [
+                jnp.dot(rows[s], cols[layer, (y + hop) % NY], preferred_element_type=f32) for _u, layer, hop in places
+            ]
+            for (u, _layer, _hop), acc in zip(places, accs):
+                if starts:
+                    sbuf[s, u] = acc.astype(bf16)
+                    ring_copy(s, u, way).start()
+                else:
+                    own[s, u] = acc
+
+        def two(k, carry):
+            some(first + 2 * k, 2)
             return carry
 
-        lax.fori_loop(first, last, one, 0)
+        many = jnp.maximum(last - first, 0)
+        lax.fori_loop(0, many // 2, two, 0)
+
+        @pl.when(many % 2 == 1)
+        def _():
+            some(last - 1, 1)
 
     def add(s, p, way, first, last):
         _dest, b = place_of(s)

time: 118 us -> 118 us (level)
  no operation moved by 1% of the time
where the time goes in v4:
time: 118 us
  Pallas kernels  112 us (95%)
  other arithmetic  4.38 us (4%)
    pallas_call x1, Pallas kernels, products(): pl.pallas_call(kernel, out_shape=jax.ShapeDtypeStruct((2, 2 * NY * F, F),...  112 us

profile of v4, /device:TPU:2, one launch (start us, length us, event | category | flops | bytes accessed | tf_op | source)
XLA Modules:
  0.0 117.6 jit_solution(7704358824194296258)
XLA Ops:
  0.6 112.5 %shard_map.59 = bf16[2,2048,256]{2,1,0:T(8,128)(2,1)} custom-call(s32[4]{0:T(128)} %len_hbm.1, bf16[1024,256]{1,0:T(8,128)(2,1)} %base_hbm.1, bf16[1024,256]{1,0:T(8,128)(2,1)} %bitcast.2, f32[1,256]{1,0:T(1,128)} %bitcast.3), custom_call_target="tpu_custom_call" | custom-call | flops 8589934592 | bytes 8388608 | tf_op jit(solution)/shard_map/pallas_call | solution.py:370
  113.1 0.0 copy-start
  113.1 2.1 %convert_element_type.3 = f32[2,2048,256]{2,1,0:T(8,128)S(1)} convert(bf16[2,2048,256]{2,1,0:T(8,128)(2,1)} %shard_map.59) | non-fusion elementwise | flops 1048576 | bytes 6291456 | tf_op jit(solution)/shard_map/convert_element_type | solution.py:409
  115.2 0.1 copy-done
  115.3 2.3 %slice_select_fusion = (f32[1,2048,256]{2,1,0:T(8,128)}, f32[1,2048,256]{2,1,0:T(8,128)}) fusion(f32[2,2048,256]{2,1,0:T(8,128)S(1)} %convert_element_type.3, pred[]{:T(512)S(6)} %eq.3, bf16[2,2048,256]{2,1,0:T(8,128)(2,1)S(1)} %copy-done), kind=kLoop, calls=%fused_computation | loop fusion | flops 524288 | bytes 8388609 | tf_op jit(solution)/shard_map/jit(_where)/select_n | solution.py:411
Async XLA Ops:
  113.1 2.2 %copy-start = (bf16[2,2048,256]{2,1,0:T(8,128)(2,1)S(1)}, bf16[2,2048,256]{2,1,0:T(8,128)(2,1)}, u32[]{:S(2)}) copy-start(bf16[2,2048,256]{2,1,0:T(8,128)(2,1)} %shard_map.59) | copy-start | bytes 6291460
